TPU v7x, 256 devices: a whole 4x4x8 slice. The times are simulated.
256 devices in a mesh: seq: 32 (over z, x), fsdp: 8 (over y, core).
Axes of the slice: x: 4, y: 4, z: 8, core: 2. Of those that a mesh axis runs over, the one named last changes fastest.
Arguments:
- query_in: bfloat16 [8, 4096, 5120], P('fsdp', 'seq'), may hold values from -400 to 400, as said below
- key_in: bfloat16 [8, 4096, 5120], P('fsdp', 'seq'), may hold values from -400 to 400
- value_in: bfloat16 [8, 4096, 5120], P('fsdp', 'seq'), may hold values from -24 to 24
- out_grad: bfloat16 [8, 4096, 5120], P('fsdp', 'seq'), may hold values from -24 to 24
- gain_q: bfloat16 [5120], P('fsdp'), may hold values from 0.099609375 to 1.8984375
- gain_k: bfloat16 [5120], P('fsdp'), may hold values from 0.099609375 to 1.8984375
- mask_lists: int32 [40, 32, 11], replicated, may hold values from 0 to 31, as said below
- tile_counts: int32 [40, 32], replicated, may hold values from 1 to 11
- head_slot: int32 [40], replicated, may hold values from 0 to 63, as said below
Outputs:
- attn_out: bfloat16 [8, 4096, 5120], P('fsdp', 'seq')
- lse_slots: float32 [8, 64, 4096], P('fsdp', 'seq')
- grad_q: bfloat16 [8, 4096, 5120], P('fsdp', 'seq')
- grad_k: bfloat16 [8, 4096, 5120], P('fsdp', 'seq')
- grad_v: bfloat16 [8, 4096, 5120], P('fsdp', 'seq')
- grad_gain_q: float32 [5120], P('fsdp')
- grad_gain_k: float32 [5120], P('fsdp')
Inputs may be any that keep to these rules, and one draw needn't show every extreme that they name: query_in and key_in are finite. `mask_lists`: for head h and query tile i, entries 0 to tile_counts[h, i] - 1 name distinct key tiles in increasing order, tile i among them; the entries after them are ignored. `head_slot`: the 40 heads have distinct slots; slot s belongs to the device of index s // 2 along seq; every device along seq holds between 1 and 2 heads, some device holding 2.
All inputs are finite; a program needn't handle non-finite values.
Results may differ from a plain program's by a relative error of at most 0.035.
The roundings to bfloat16 on the way count: a program that leaves them out, or rounds other values in their place, can miss the bound.
Values may be sent and summed in bfloat16 or wider, within the bound.
No kernel may reach another device: no remote copies, remote signals or barrier semaphores. Data moves between devices by JAX's collectives and lax.ppermute only.
A program may use at most 128 MiB of HBM per device.

v0:
```python
import math

import jax
import jax.numpy as jnp
from jax import lax
from jax.sharding import PartitionSpec as P

norm_eps = 1e-06


def normalize(values, gain_vec):
    as_float = values.astype(jnp.float32)
    inverse = lax.rsqrt(jnp.mean(as_float * as_float, axis=-1, keepdims=True) + norm_eps)
    return ((as_float * inverse * gain_vec.astype(jnp.float32)).astype(jnp.bfloat16), inverse)


def norm_backward(values, inverse, gain_vec, upstream):
    as_float = values.astype(jnp.float32)
    incoming = upstream.astype(jnp.float32)
    weighted = incoming * gain_vec.astype(jnp.float32)
    inner_mean = jnp.mean(weighted * as_float, axis=-1, keepdims=True)
    grad_in = inverse * weighted - as_float * (inverse * inverse * inverse) * inner_mean
    gain_term = jnp.sum(incoming * as_float * inverse, axis=(0, 1))
    return (grad_in.astype(jnp.bfloat16), gain_term)


def block_group():
    return 4


def masked_scores(query_tiles, key_tiles, counts_blk, score_scale):
    scores = (
        jnp.einsum("gid,gkjd->gikj", query_tiles, key_tiles, preferred_element_type=jnp.float32)
        * score_scale
    )
    usable = jnp.arange(key_tiles.shape[1], dtype=jnp.int32)[None, :] < counts_blk[:, None]
    return jnp.where(usable[:, None, :, None], scores, -jnp.inf)


def head_forward(query_head, key_head, value_head, tile_lists, counts):
    count_tiles, listed = tile_lists.shape
    head_width = query_head.shape[1]
    tile_rows = query_head.shape[0] // count_tiles
    tile_group = block_group()
    blocks = count_tiles // tile_group
    score_scale = 1.0 / math.sqrt(head_width)
    key_tiles_all = key_head.reshape(count_tiles, tile_rows, head_width)
    value_tiles_all = value_head.reshape(count_tiles, tile_rows, head_width)

    def block_step(pieces):
        query_tiles, lists_blk, counts_blk = pieces
        key_tiles = jnp.take(key_tiles_all, lists_blk, axis=0)
        value_tiles = jnp.take(value_tiles_all, lists_blk, axis=0)
        scores = masked_scores(query_tiles, key_tiles, counts_blk, score_scale)
        row_max = jnp.max(scores, axis=(2, 3), keepdims=True)
        row_total = jnp.sum(jnp.exp(scores - row_max), axis=(2, 3), keepdims=True)
        log_total = row_max + jnp.log(row_total)
        weights = jnp.exp(scores - log_total).astype(jnp.bfloat16)
        result = jnp.einsum(
            "gikj,gkjd->gid", weights, value_tiles, preferred_element_type=jnp.float32
        )
        return (result.astype(jnp.bfloat16), log_total[:, :, 0, 0])

    result, log_total = lax.map(
        block_step,
        (
            query_head.reshape(blocks, tile_group, tile_rows, head_width),
            tile_lists.reshape(blocks, tile_group, listed),
            counts.reshape(blocks, tile_group),
        ),
    )
    return (result.reshape(-1, head_width), log_total.reshape(-1))


def head_backward(
    query_head, key_head, value_head, result_head, grad_head, log_total, tile_lists, counts
):
    count_tiles, listed = tile_lists.shape
    head_width = query_head.shape[1]
    tile_rows = query_head.shape[0] // count_tiles
    tile_group = block_group()
    blocks = count_tiles // tile_group
    score_scale = 1.0 / math.sqrt(head_width)
    key_tiles_all = key_head.reshape(count_tiles, tile_rows, head_width)
    value_tiles_all = value_head.reshape(count_tiles, tile_rows, head_width)

    def shaped(values):
        return values.reshape(blocks, tile_group, tile_rows, head_width)

    def block_step(carried, pieces):
        key_grad, value_grad = carried
        query_tiles, result_tiles, grad_tiles, total_blk, lists_blk, counts_blk = pieces
        key_tiles = jnp.take(key_tiles_all, lists_blk, axis=0)
        value_tiles = jnp.take(value_tiles_all, lists_blk, axis=0)
        scores = masked_scores(query_tiles, key_tiles, counts_blk, score_scale)
        weights = jnp.exp(scores - total_blk[:, :, None, None])
        row_delta = jnp.sum(
            grad_tiles.astype(jnp.float32) * result_tiles.astype(jnp.float32), axis=-1
        )
        prob_grad = jnp.einsum(
            "gid,gkjd->gikj", grad_tiles, value_tiles, preferred_element_type=jnp.float32
        )
        dscore = (weights * (prob_grad - row_delta[:, :, None, None])).astype(jnp.bfloat16)
        query_grad = (
            jnp.einsum("gikj,gkjd->gid", dscore, key_tiles, preferred_element_type=jnp.float32)
            * score_scale
        )
        key_part = (
            jnp.einsum("gikj,gid->gkjd", dscore, query_tiles, preferred_element_type=jnp.float32)
            * score_scale
        )
        value_part = jnp.einsum(
            "gikj,gid->gkjd",
            weights.astype(jnp.bfloat16),
            grad_tiles,
            preferred_element_type=jnp.float32,
        )
        key_grad = key_grad.at[lists_blk].add(key_part)
        value_grad = value_grad.at[lists_blk].add(value_part)
        return ((key_grad, value_grad), query_grad.astype(jnp.bfloat16))

    zero_tiles = jnp.zeros((count_tiles, tile_rows, head_width), jnp.float32)
    (key_grad, value_grad), query_grad = lax.scan(
        block_step,
        (zero_tiles, zero_tiles),
        (
            shaped(query_head),
            shaped(result_head),
            shaped(grad_head),
            log_total.reshape(blocks, tile_group, tile_rows),
            tile_lists.reshape(blocks, tile_group, listed),
            counts.reshape(blocks, tile_group),
        ),
    )
    return (
        query_grad.reshape(-1, head_width),
        key_grad.reshape(-1, head_width).astype(jnp.bfloat16),
        value_grad.reshape(-1, head_width).astype(jnp.bfloat16),
    )


def owner_forward(query_own, key_own, value_own, slot_heads, slot_live, mask_lists, tile_counts):
    clip_count, depth_here, seq_rows, head_width = query_own.shape
    flat_count = clip_count * depth_here
    head_ids = jnp.tile(slot_heads, clip_count)
    live_flags = jnp.tile(slot_live, clip_count)

    def per_slot(pieces):
        query_head, key_head, value_head, head_id, is_live = pieces

        def compute():
            return head_forward(
                query_head, key_head, value_head, mask_lists[head_id], tile_counts[head_id]
            )

        def skipped():
            return (jnp.zeros_like(query_head), jnp.zeros((seq_rows,), jnp.float32))

        return lax.cond(is_live, compute, skipped)

    result, log_total = lax.map(
        per_slot,
        (
            query_own.reshape(flat_count, seq_rows, head_width),
            key_own.reshape(flat_count, seq_rows, head_width),
            value_own.reshape(flat_count, seq_rows, head_width),
            head_ids,
            live_flags,
        ),
    )
    return (
        result.reshape(clip_count, depth_here, seq_rows, head_width),
        log_total.reshape(clip_count, depth_here, seq_rows),
    )


def owner_backward(
    query_own,
    key_own,
    value_own,
    result_own,
    grad_own,
    total_own,
    slot_heads,
    slot_live,
    mask_lists,
    tile_counts,
):
    clip_count, depth_here, seq_rows, head_width = query_own.shape
    flat_count = clip_count * depth_here
    head_ids = jnp.tile(slot_heads, clip_count)
    live_flags = jnp.tile(slot_live, clip_count)

    def flat(values):
        return values.reshape(flat_count, seq_rows, head_width)

    def per_slot(pieces):
        query_head, key_head, value_head, result_head, grad_head, total_head, head_id, is_live = (
            pieces
        )

        def compute():
            return head_backward(
                query_head,
                key_head,
                value_head,
                result_head,
                grad_head,
                total_head,
                mask_lists[head_id],
                tile_counts[head_id],
            )

        def skipped():
            return (
                jnp.zeros_like(query_head),
                jnp.zeros_like(query_head),
                jnp.zeros_like(query_head),
            )

        return lax.cond(is_live, compute, skipped)

    query_grad, key_grad, value_grad = lax.map(
        per_slot,
        (
            flat(query_own),
            flat(key_own),
            flat(value_own),
            flat(result_own),
            flat(grad_own),
            total_own.reshape(flat_count, seq_rows),
            head_ids,
            live_flags,
        ),
    )
    final_shape = (clip_count, depth_here, seq_rows, head_width)
    return (
        query_grad.reshape(final_shape),
        key_grad.reshape(final_shape),
        value_grad.reshape(final_shape),
    )


def shards(
    query_in, key_in, value_in, out_grad, gain_q, gain_k, mask_lists, tile_counts, head_slot
):
    seq_devices = lax.axis_size("seq")
    fsdp_devices = lax.axis_size("fsdp")
    own_index = lax.axis_index("seq")
    head_count = mask_lists.shape[0]
    clip_count, token_count, feature_count = query_in.shape
    head_width = feature_count // head_count
    slot_depth = (head_count + seq_devices - 1) // seq_devices
    slot_total = seq_devices * slot_depth
    gains_query, gains_key = (
        lax.all_gather(gain_q, "fsdp", axis=0, tiled=True),
        lax.all_gather(gain_k, "fsdp", axis=0, tiled=True),
    )
    query_norm, query_inv = normalize(query_in, gains_query)
    key_norm, key_inv = normalize(key_in, gains_key)
    placing = head_slot[None, :] == jnp.arange(slot_total, dtype=jnp.int32)[:, None]
    place_bf = placing.astype(jnp.bfloat16)

    def slot_order(values):
        split_heads = values.reshape(clip_count, token_count, head_count, head_width)
        return jnp.einsum(
            "cthd,sh->cstd", split_heads, place_bf, preferred_element_type=jnp.float32
        ).astype(jnp.bfloat16)

    def head_order(values):
        merged = jnp.einsum("cstd,sh->cthd", values, place_bf, preferred_element_type=jnp.float32)
        return merged.reshape(clip_count, token_count, feature_count).astype(jnp.bfloat16)

    heads_index = jnp.arange(head_count, dtype=jnp.int32)
    own_slots = own_index * slot_depth + jnp.arange(slot_depth, dtype=jnp.int32)
    own_match = head_slot[None, :] == own_slots[:, None]
    own_heads = jnp.sum(jnp.where(own_match, heads_index[None, :], 0), axis=1)
    own_live = jnp.any(own_match, axis=1)
    send_query = slot_order(query_norm)
    send_key = slot_order(key_norm)
    send_value = slot_order(value_in)
    query_own, key_own, value_own = (
        lax.all_to_all(send_query, "seq", split_axis=1, concat_axis=2, tiled=True),
        lax.all_to_all(send_key, "seq", split_axis=1, concat_axis=2, tiled=True),
        lax.all_to_all(send_value, "seq", split_axis=1, concat_axis=2, tiled=True),
    )
    result_own, total_own = owner_forward(
        query_own, key_own, value_own, own_heads, own_live, mask_lists, tile_counts
    )
    attn_out = head_order(
        lax.all_to_all(result_own, "seq", split_axis=2, concat_axis=1, tiled=True)
    )
    grad_own = lax.all_to_all(slot_order(out_grad), "seq", split_axis=1, concat_axis=2, tiled=True)
    dq_own, dk_own, dv_own = owner_backward(
        query_own,
        key_own,
        value_own,
        result_own,
        grad_own,
        total_own,
        own_heads,
        own_live,
        mask_lists,
        tile_counts,
    )
    dq_back, dk_back, dv_back = (
        lax.all_to_all(dq_own, "seq", split_axis=2, concat_axis=1, tiled=True),
        lax.all_to_all(dk_own, "seq", split_axis=2, concat_axis=1, tiled=True),
        lax.all_to_all(dv_own, "seq", split_axis=2, concat_axis=1, tiled=True),
    )
    grad_q, term_q = norm_backward(query_in, query_inv, gains_query, head_order(dq_back))
    grad_k, term_k = norm_backward(key_in, key_inv, gains_key, head_order(dk_back))
    grad_v = head_order(dv_back)
    total_q, total_k = (
        lax.psum(term_q.astype(jnp.bfloat16), "seq").astype(jnp.float32),
        lax.psum(term_k.astype(jnp.bfloat16), "seq").astype(jnp.float32),
    )
    share_q, share_k = (
        lax.psum_scatter(
            total_q.astype(jnp.bfloat16), "fsdp", scatter_dimension=0, tiled=True
        ).astype(jnp.float32),
        lax.psum_scatter(
            total_k.astype(jnp.bfloat16), "fsdp", scatter_dimension=0, tiled=True
        ).astype(jnp.float32),
    )
    factor = 1.0 / math.sqrt(fsdp_devices * clip_count * token_count * seq_devices)
    return (attn_out, total_own, grad_q, grad_k, grad_v, share_q * factor, share_k * factor)


def solution(mesh):
    in_specs = (
        P("fsdp", "seq", None),
        P("fsdp", "seq", None),
        P("fsdp", "seq", None),
        P("fsdp", "seq", None),
        P("fsdp"),
        P("fsdp"),
        P(),
        P(),
        P(),
    )
    out_specs = (
        P("fsdp", "seq", None),
        P("fsdp", "seq", None),
        P("fsdp", "seq", None),
        P("fsdp", "seq", None),
        P("fsdp", "seq", None),
        P("fsdp"),
        P("fsdp"),
    )
    return jax.shard_map(shards, mesh=mesh, in_specs=in_specs, out_specs=out_specs, check_vma=False)
```

profile of v0, /device:TPU:4, one launch (start us, length us, event | category | flops | bytes accessed | tf_op | source)
XLA Modules:
  0.0 1262.0 jit_solution(1452652852043481398)
XLA Ops:
  3.7 13.1 %all-gather = bf16[8,1,640]{2,1,0:T(2,128)(2,1)S(1)} all-gather(bf16[1,1,640]{2,1,0:T(2,128)(2,1)S(1)} %reshape.694), channel_id=1, replica_groups=mesh['seq'=32,'fsdp'=8] {'fsdp'}, dimensions={0}, use_global_device_ids=true | all-gather | bytes 11520 | tf_op jit(solution)/shard_map/all_gather | solution.py:256
  21.2 11.7 all-to-all-start
  32.9 12.6 %all-gather.1 = bf16[8,1,640]{2,1,0:T(2,128)(2,1)S(1)} all-gather(bf16[1,1,640]{2,1,0:T(2,128)(2,1)S(1)} %reshape.696), channel_id=1, replica_groups=mesh['seq'=32,'fsdp'=8] {'fsdp'}, dimensions={0}, use_global_device_ids=true | all-gather | bytes 11520 | tf_op jit(solution)/shard_map/all_gather | solution.py:257
  51.3 31.3 %all-to-all-done = bf16[1,64,128,128]{3,2,0,1:T(8,128)(2,1)S(1)} async-done(((bf16[1,64,128,128]{3,2,0,1:T(8,128)(2,1)}), bf16[1,64,128,128]{3,2,0,1:T(8,128)(2,1)S(1)}, u32[]{:S(2)}, u32[]{:S(2)}) %all-to-all-start) | async-done | bytes 2097184 | tf_op jit(solution)/shard_map/all_to_all | solution.py:283
  92.7 46.0 %all-to-all-done.1 = bf16[1,64,128,128]{3,2,0,1:T(8,128)(2,1)} async-done(((bf16[1,64,128,128]{3,2,0,1:T(8,128)(2,1)}), bf16[1,64,128,128]{3,2,0,1:T(8,128)(2,1)}, u32[]{:S(2)}, u32[]{:S(2)}) %all-to-all-start.1) | async-done | bytes 2097184 | tf_op jit(solution)/shard_map/all_to_all | solution.py:284
  149.7 45.7 %all-to-all-done.2 = bf16[1,64,128,128]{3,2,0,1:T(8,128)(2,1)} async-done(((bf16[1,64,128,128]{3,2,0,1:T(8,128)(2,1)}), bf16[1,64,128,128]{3,2,0,1:T(8,128)(2,1)}, u32[]{:S(2)}, u32[]{:S(2)}) %all-to-all-start.2) | async-done | bytes 2097184 | tf_op jit(solution)/shard_map/all_to_all | solution.py:285
  213.5 170.1 %while.70 = (s32[]{:T(128)}, bf16[2,4096,128]{2,1,0:T(8,128)(2,1)}, f32[2,4096]{1,0:T(2,128)}, pred[2]{0:T(512)(128)(4,1)S(1)}, bf16[2,4096,128]{2,1,0:T(8,128)(...) while((s32[]{:T(128)}, bf16[2,4096,128]{2,1,0:T(8,128)(2,1)}, ...), condition=%wide.region_11.13_spmd, body=%wide.region_4.12_spmd.sunk | while | flops 378536768 | bytes 34400104 | solution.py:161
  214.8 80.1 %conditional.4 = (bf16[1,4096,128]{2,1,0:T(8,128)(2,1)}, f32[1,4096]{1,0:T(1,128)}) conditional(s32[]{:T(128)} %bitcast.246, () %tuple.124, (bf16[2,4096,128]{2,1,0:T(8,128)(2,1)}, s32[]{:T(128)}, s32[2]{0:T(128)}, s32[40,32,11]{2,1,0:T(8,128)}, s32[40,32]{1,0:T(8,128)}, /*index=5*/bf16[2,4096,128]{2,1,0:T(8,128)(2,1)}, ...), branch_computations={%region_5.5_spmd, %region_6.11_spmd} | conditional | flops 378536768 | bytes 32269414 | solution.py:159
  223.9 71.0 %while.68 = (s32[]{:T(128)}, bf16[8,4,128,128]{3,2,1,0:T(8,128)(2,1)}, f32[8,4,128]{2,1,0:T(4,128)}, s32[8,4]{1,0:T(8,128)S(1)}, bf16[8,4,128,128]{3,2,1,0:T(8,1...) while((s32[]{:T(128)}, ...), condition=%wide.region_10.10_spmd, body=%wide.region_7.9_spmd.sunk | while | flops 378536768 | bytes 17585836 | solution.py:64
  299.8 80.1 %conditional.4 = (bf16[1,4096,128]{2,1,0:T(8,128)(2,1)}, f32[1,4096]{1,0:T(1,128)}) conditional(s32[]{:T(128)} %bitcast.246, () %tuple.124, (bf16[2,4096,128]{2,1,0:T(8,128)(2,1)}, s32[]{:T(128)}, s32[2]{0:T(128)}, s32[40,32,11]{2,1,0:T(8,128)}, s32[40,32]{1,0:T(8,128)}, /*index=5*/bf16[2,4096,128]{2,1,0:T(8,128)(2,1)}, ...), branch_computations={%region_5.5_spmd, %region_6.11_spmd} | conditional | flops 378536768 | bytes 32269414 | solution.py:159
  308.9 71.0 %while.68 = (s32[]{:T(128)}, bf16[8,4,128,128]{3,2,1,0:T(8,128)(2,1)}, f32[8,4,128]{2,1,0:T(4,128)}, s32[8,4]{1,0:T(8,128)S(1)}, bf16[8,4,128,128]{3,2,1,0:T(8,1...) while((s32[]{:T(128)}, ...), condition=%wide.region_10.10_spmd, body=%wide.region_7.9_spmd.sunk | while | flops 378536768 | bytes 17585836 | solution.py:64
  405.3 577.2 %while.71 = (s32[]{:T(128)}, bf16[2,4096,128]{2,1,0:T(8,128)(2,1)}, bf16[2,4096,128]{2,1,0:T(8,128)(2,1)}, bf16[2,4096,128]{2,1,0:T(8,128)(2,1)}, pred[2]{0:T(51...) while((s32[]{:T(128)}, bf16[2,4096,128]{2,1,0:T(8,128)(2,1)}, ...), condition=%wide.region_20.22_spmd, body=%wide.region_12.21_spmd.sunk | while | flops 935723968 | bytes 105307768 | solution.py:223
  406.5 280.7 %conditional.5 = (bf16[1,4096,128]{2,1,0:T(8,128)(2,1)}, bf16[1,4096,128]{2,1,0:T(8,128)(2,1)}, bf16[1,4096,128]{2,1,0:T(8,128)(2,1)}) conditional(s32[]{:T(128)} %bitcast.247, () %tuple.128, (bf16[2,4096,128]{2,1,0:T(8,128)(2,1)}, s32[]{:T(128)}, bf16[2,4096,128]{2,1,0:T(8,128)(2,1)}, bf16[2,4096,128]{2,1,0:T(8,128)(2,1)}, ...), branch_computations={%region_13.14_spmd, %region_14.20_spmd} | conditional | flops 935723968 | bytes 82237712 | solution.py:221
  422.6 260.6 %while.69 = (s32[]{:T(128)}, f32[32,128,128]{2,1,0:T(8,128)}, f32[32,128,128]{2,1,0:T(8,128)}, bf16[8,4,128,128]{3,2,1,0:T(8,128)(2,1)}, s32[8,4,11]{2,1,0:T(4,1...) while((s32[]{:T(128)}, f32[32,128,128]{2,1,0:T(8,128)}, ...), condition=%wide.region_19.19_spmd, body=%wide.region_15.18_spmd.sunk | while | flops 934675392 | bytes 52841244 | solution.py:123
  478.6 9.0 scatter_fusion
  543.9 9.0 scatter_fusion
  598.1 9.0 scatter_fusion.1
  609.1 9.0 scatter_fusion
  694.9 281.1 %conditional.5 = (bf16[1,4096,128]{2,1,0:T(8,128)(2,1)}, bf16[1,4096,128]{2,1,0:T(8,128)(2,1)}, bf16[1,4096,128]{2,1,0:T(8,128)(2,1)}) conditional(s32[]{:T(128)} %bitcast.247, () %tuple.128, (bf16[2,4096,128]{2,1,0:T(8,128)(2,1)}, s32[]{:T(128)}, bf16[2,4096,128]{2,1,0:T(8,128)(2,1)}, bf16[2,4096,128]{2,1,0:T(8,128)(2,1)}, ...), branch_computations={%region_13.14_spmd, %region_14.20_spmd} | conditional | flops 935723968 | bytes 82237712 | solution.py:221
  711.0 261.0 %while.69 = (s32[]{:T(128)}, f32[32,128,128]{2,1,0:T(8,128)}, f32[32,128,128]{2,1,0:T(8,128)}, bf16[8,4,128,128]{3,2,1,0:T(8,128)(2,1)}, s32[8,4,11]{2,1,0:T(4,1...) while((s32[]{:T(128)}, f32[32,128,128]{2,1,0:T(8,128)}, ...), condition=%wide.region_19.19_spmd, body=%wide.region_15.18_spmd.sunk | while | flops 934675392 | bytes 52841244 | solution.py:123
  723.7 9.0 scatter_fusion.1
  734.8 9.0 scatter_fusion
  756.5 9.0 scatter_fusion.1
  821.7 9.0 scatter_fusion.1
  832.8 9.0 scatter_fusion
  865.4 9.0 scatter_fusion
  930.6 9.0 scatter_fusion
  1001.3 41.6 %all-to-all-done.7 = bf16[1,2,4096,128]{3,1,0,2:T(2,128)(2,1)S(1)} async-done(((bf16[1,2,4096,128]{3,1,0,2:T(2,128)(2,1)}), bf16[1,2,4096,128]{3,1,0,2:T(2,128)(2,1)S(1)}, u32[]{:S(2)}, u32[]{:S(2)}) %all-to-all-start.7) | async-done | bytes 2097184 | tf_op jit(solution)/shard_map/all_to_all | solution.py:309
  1055.0 41.4 %all-to-all-done.5 = bf16[1,2,4096,128]{3,1,0,2:T(2,128)(2,1)} async-done(((bf16[1,2,4096,128]{3,1,0,2:T(2,128)(2,1)}), bf16[1,2,4096,128]{3,1,0,2:T(2,128)(2,1)}, u32[]{:S(2)}, u32[]{:S(2)}) %all-to-all-start.5) | async-done | bytes 2097184 | tf_op jit(solution)/shard_map/all_to_all | solution.py:307
  1123.3 26.9 %all-to-all-done.6 = bf16[1,2,4096,128]{3,1,0,2:T(2,128)(2,1)} async-done(((bf16[1,2,4096,128]{3,1,0,2:T(2,128)(2,1)}), bf16[1,2,4096,128]{3,1,0,2:T(2,128)(2,1)}, u32[]{:S(2)}, u32[]{:S(2)}) %all-to-all-start.6) | async-done | bytes 2097184 | tf_op jit(solution)/shard_map/all_to_all | solution.py:308
  1164.3 23.6 %all-reduce.3 = (bf16[5120]{0:T(1024)(128)(2,1)S(1)}, bf16[5120]{0:T(1024)(128)(2,1)S(1)}) all-reduce(bf16[5120]{0:T(1024)(128)(2,1)S(1)} %get-tuple-element.534, bf16[5120]{0:T(1024)(128)(2,1)S(1)} %get-tuple-element.651), channel_id=2, replica_groups=mesh['seq'=32,'fsdp'=8] {'fsdp'}, use_global_device_ids=true, to_apply=%region_25.27.clone | all-reduce | flops 10240 | bytes 40960
  1188.1 67.1 %all-reduce.2 = (bf16[640]{0:T(1024)(128)(2,1)S(1)}, bf16[640]{0:T(1024)(128)(2,1)S(1)}) all-reduce(bf16[640]{0:T(1024)(128)(2,1)S(1)} %dynamic-slice.1, bf16[640]{0:T(1024)(128)(2,1)S(1)} %dynamic-slice.3), channel_id=1, replica_groups=mesh['seq'=32,'fsdp'=8] {'seq'}, use_global_device_ids=true, to_apply=%region_24.26 | all-reduce | flops 1280 | bytes 5120 | tf_op jit(solution)/shard_map/psum | solution.py:315
  (656 shorter events, 788.0 us)
Async XLA Ops:
  0.6 16.2 %copy-start.4 = (bf16[1,128,5120]{2,1,0:T(8,128)(2,1)S(1)}, bf16[1,128,5120]{2,1,0:T(8,128)(2,1)}, u32[]{:S(2)}) copy-start(bf16[1,128,5120]{2,1,0:T(8,128)(2,1)} %param.23) | copy-start | bytes 3932164
  3.0 14.6 %copy-start.20 = (f32[128]{0:T(128)}, f32[128]{0:T(128)S(1)}, u32[]{:S(2)}) copy-start(f32[128]{0:T(128)S(1)} %get-tuple-element.649) | copy-start | bytes 1540
  21.2 11.7 copy-start.24
  21.2 24.4 %copy-start.5 = (bf16[1,128,5120]{2,1,0:T(8,128)(2,1)S(1)}, bf16[1,128,5120]{2,1,0:T(8,128)(2,1)}, u32[]{:S(2)}) copy-start(bf16[1,128,5120]{2,1,0:T(8,128)(2,1)} %param.24) | copy-start | bytes 3932164
  21.2 61.5 %all-to-all-start = ((bf16[1,64,128,128]{3,2,0,1:T(8,128)(2,1)}), bf16[1,64,128,128]{3,2,0,1:T(8,128)(2,1)S(1)}, u32[]{:S(2)}, u32[]{:S(2)}) async-start(bf16[1,64,128,128]{3,2,0,1:T(8,128)(2,1)} %copy.72), calls=%async_computation | async-start | bytes 4194304 | tf_op jit(solution)/shard_map/all_to_all | solution.py:283
  51.3 37.6 %copy-start.9 = (bf16[1,128,5120]{2,1,0:T(8,128)(2,1)S(1)}, bf16[1,128,5120]{2,1,0:T(8,128)(2,1)}, u32[]{:S(2)}) copy-start(bf16[1,128,5120]{2,1,0:T(8,128)(2,1)} %param.25) | copy-start | bytes 3932164
  82.7 56.1 %all-to-all-start.1 = ((bf16[1,64,128,128]{3,2,0,1:T(8,128)(2,1)}), bf16[1,64,128,128]{3,2,0,1:T(8,128)(2,1)}, u32[]{:S(2)}, u32[]{:S(2)}) async-start(bf16[1,64,128,128]{3,2,0,1:T(8,128)(2,1)} %copy.74), calls=%async_computation.1 | async-start | bytes 4194304 | tf_op jit(solution)/shard_map/all_to_all | solution.py:284
  92.7 53.2 %copy-start.10 = (bf16[1,128,5120]{2,1,0:T(8,128)(2,1)S(1)}, bf16[1,128,5120]{2,1,0:T(8,128)(2,1)}, u32[]{:S(2)}) copy-start(bf16[1,128,5120]{2,1,0:T(8,128)(2,1)} %param.26) | copy-start | bytes 3932164
  138.8 56.6 %all-to-all-start.2 = ((bf16[1,64,128,128]{3,2,0,1:T(8,128)(2,1)}), bf16[1,64,128,128]{3,2,0,1:T(8,128)(2,1)}, u32[]{:S(2)}, u32[]{:S(2)}) async-start(bf16[1,64,128,128]{3,2,0,1:T(8,128)(2,1)} %copy.76), calls=%async_computation.2 | async-start | bytes 4194304 | tf_op jit(solution)/shard_map/all_to_all | solution.py:285
  149.7 51.3 %copy-start.19 = (s32[40,32]{0,1:T(8,128)S(1)}, s32[40,32]{0,1:T(8,128)}, u32[]{:S(2)}) copy-start(s32[40,32]{0,1:T(8,128)} %param.30) | copy-start | bytes 15364
  149.7 52.0 %copy-start.16 = (s32[40,32,11]{0,1,2:T(8,128)S(1)}, s32[40,32,11]{0,1,2:T(8,128)}, u32[]{:S(2)}) copy-start(s32[40,32,11]{0,1,2:T(8,128)} %param.29) | copy-start | bytes 168964
  195.4 194.0 %all-to-all-start.4 = ((bf16[1,64,128,128]{3,2,0,1:T(8,128)(2,1)}), bf16[1,64,128,128]{3,2,0,1:T(8,128)(2,1)}, u32[]{:S(2)}, u32[]{:S(2)}) async-start(bf16[1,64,128,128]{3,2,0,1:T(8,128)(2,1)} %copy.82), calls=%async_computation.4 | async-start | bytes 4194304 | tf_op jit(solution)/shard_map/all_to_all | solution.py:293
  294.9 3.7 copy-start.29
  379.9 3.8 copy-start.29
  389.5 598.8 %all-to-all-start.3 = ((bf16[1,2,4096,128]{3,1,0,2:T(2,128)(2,1)}), bf16[1,2,4096,128]{3,1,0,2:T(2,128)(2,1)}, u32[]{:S(2)}, u32[]{:S(2)}) async-start(bf16[1,2,4096,128]{3,1,0,2:T(2,128)(2,1)} %bitcast.219), calls=%async_computation.3 | async-start | bytes 4194304 | tf_op jit(solution)/shard_map/all_to_all | solution.py:291
  402.1 3.2 copy-start.15
  683.2 2.9 copy-start
  689.7 4.0 copy-start.31
  978.4 4.0 copy-start.31
  988.3 54.6 %all-to-all-start.7 = ((bf16[1,2,4096,128]{3,1,0,2:T(2,128)(2,1)}), bf16[1,2,4096,128]{3,1,0,2:T(2,128)(2,1)S(1)}, u32[]{:S(2)}, u32[]{:S(2)}) async-start(bf16[1,2,4096,128]{3,1,0,2:T(2,128)(2,1)} %bitcast.291), calls=%async_computation.7 | async-start | bytes 4194304 | tf_op jit(solution)/shard_map/all_to_all | solution.py:309
  1042.9 53.5 %all-to-all-start.5 = ((bf16[1,2,4096,128]{3,1,0,2:T(2,128)(2,1)}), bf16[1,2,4096,128]{3,1,0,2:T(2,128)(2,1)}, u32[]{:S(2)}, u32[]{:S(2)}) async-start(bf16[1,2,4096,128]{3,1,0,2:T(2,128)(2,1)} %bitcast.290), calls=%async_computation.5 | async-start | bytes 4194304 | tf_op jit(solution)/shard_map/all_to_all | solution.py:307
  1096.4 6.8 copy-start.27
  1096.4 53.8 %all-to-all-start.6 = ((bf16[1,2,4096,128]{3,1,0,2:T(2,128)(2,1)}), bf16[1,2,4096,128]{3,1,0,2:T(2,128)(2,1)}, u32[]{:S(2)}, u32[]{:S(2)}) async-start(bf16[1,2,4096,128]{3,1,0,2:T(2,128)(2,1)} %bitcast.289), calls=%async_computation.6 | async-start | bytes 4194304 | tf_op jit(solution)/shard_map/all_to_all | solution.py:308
  1104.4 4.0 copy-start.18
  1156.2 3.5 copy-start.12
  1156.2 3.5 copy-start.14
  1156.2 3.5 copy-start.21
  1156.2 3.5 copy-start.23
  1159.8 96.7 %copy-start.25 = (f32[128]{0:T(128)S(1)}, f32[128]{0:T(128)}, u32[]{:S(2)}) copy-start(f32[128]{0:T(128)} %get-tuple-element.648) | copy-start | bytes 1540
  1256.4 3.3 copy-start.3
  1256.4 3.3 copy-start.6
  1256.4 3.3 copy-start.26
  (31 other events, 44.1 us)
where the time goes:
time: 1290 us; the launch traced here: 1260 us
  other arithmetic  363 us (28%)
  local copies, waits for them, and re-layouts  259 us (20%)
  waiting for transfers between devices  233 us (18%)
  matrix products  218 us (17%)
  blocking collectives  117 us (9%)
  starting transfers between devices  58.8 us (5%)
    scatter-add x16, other arithmetic, block_step(): key_grad = key_grad.at[lists_blk].add(key_part)  143 us
    scatter-add x16, other arithmetic, block_step(): value_grad = value_grad.at[lists_blk].add(value_part)  143 us
    psum x1, blocking collectives, shards(): lax.psum(term_q.astype(jnp.bfloat16), 'seq').astype(jnp.float32)  67.1 us
    gather x32, local copies, waits for them, and re-layouts, block_step(): key_tiles = jnp.take(key_tiles_all, lists_blk, axis=0)  64 us
    dot_general x32, matrix products, masked_scores(): jnp.einsum('gid,gkjd->gikj', query_tiles, key_tiles, preferred_element_ty...  59.6 us
    all_to_all x1, waiting for transfers between devices, shards(): lax.all_to_all(send_key, 'seq', split_axis=1, concat_axis=2, tiled=True)  46 us
    gather x32, local copies, waits for them, and re-layouts, block_step(): value_tiles = jnp.take(value_tiles_all, lists_blk, axis=0)  46 us
    all_to_all x1, waiting for transfers between devices, shards(): lax.all_to_all(send_value, 'seq', split_axis=1, concat_axis=2, tiled=True)  45.7 us
  transfers between devices with their start and end apart: 8, of which 6 were waited for; matrix products, arithmetic and copies ran while one was open for 64% of the time, Pallas kernels for 0%

commit v1 on v0

v1 whole, which is shorter than its diff:
```python
import functools
import math

import jax
import jax.numpy as jnp
from jax import lax
from jax.experimental import pallas as pl
from jax.experimental.pallas import tpu as pltpu
from jax.sharding import Mesh, PartitionSpec as P

norm_eps = 1e-06
head_width = 128
tile_rows = 128
block = (tile_rows, head_width)
log2e = 1.4426950408889634
ln2 = 0.6931471805599453
masked_out = -1e30
unrolled = 4
vmem_bytes = 26 * 2**20

bf16 = jnp.bfloat16
f32 = jnp.float32
i32 = jnp.int32

vmem = pl.BlockSpec(memory_space=pltpu.VMEM)
smem = pl.BlockSpec(memory_space=pltpu.SMEM)


def dot(a, b, contract):
    dims = ((contract[:1], contract[1:]), ((), ()))
    return lax.dot_general(a, b, dims, preferred_element_type=f32)


def call(kernel, name, outs, in_specs, tiles_moved, flops=0, scratch=(), smem_outs=()):
    out_specs = tuple(smem if n in smem_outs else vmem for n in range(len(outs)))
    return pl.pallas_call(
        kernel,
        out_shape=tuple(jax.ShapeDtypeStruct(*o) for o in outs),
        in_specs=in_specs,
        out_specs=out_specs,
        scratch_shapes=list(scratch),
        compiler_params=pltpu.CompilerParams(vmem_limit_bytes=vmem_bytes),
        cost_estimate=pl.CostEstimate(
            flops=flops, bytes_accessed=tiles_moved * tile_rows * head_width * 2, transcendentals=0
        ),
        name=name,
    )


def cols(head):
    start = head * head_width
    if not isinstance(head, int):
        start = pl.multiple_of(start, head_width)
    return pl.ds(start, head_width)


def place_kernel(n_seq, heads, slot_ref, x_ref, order_ref, main_ref, held_ref):
    @pl.loop(0, 2 * n_seq)
    def _(s):
        held_ref[s] = -1

    @pl.loop(0, heads)
    def _(h):
        held_ref[slot_ref[h]] = h

    def place(position, head):
        order_ref[position] = head
        order_ref[heads + head] = position

    def step(d, used):
        low, high = held_ref[2 * d], held_ref[2 * d + 1]
        place(d, jnp.where(low >= 0, low, high))
        both = jnp.logical_and(low >= 0, high >= 0)

        @pl.when(both)
        def _():
            place(used, high)

        return used + both.astype(i32)

    lax.fori_loop(0, n_seq, step, jnp.int32(n_seq))
    for d in range(n_seq):
        main_ref[d] = x_ref[:, cols(order_ref[d])]


def split_kernel(n_seq, order_ref, x_ref, main_ref):
    for d in range(n_seq):
        main_ref[d] = x_ref[:, cols(order_ref[d])]


def norm_kernel(n_seq, heads, order_ref, q_ref, k_ref, v_ref, do_ref, gain_ref, kq_ref, extra_ref):
    for which, x_ref in ((1, q_ref), (0, k_ref)):
        total = jnp.zeros(block, f32)
        for head in range(heads):
            x = x_ref[:, cols(head)].astype(f32)
            total += x * x
        mean = jnp.sum(total, axis=1, keepdims=True) * (1.0 / (heads * head_width))
        inverse = jnp.broadcast_to(lax.rsqrt(mean + norm_eps), block)
        for p in range(heads):
            at = cols(order_ref[p])
            gain = gain_ref[1 - which : 2 - which, at].astype(f32)
            normed = (x_ref[:, at].astype(f32) * inverse * gain).astype(bf16)
            if p < n_seq:
                kq_ref[p, which] = normed
            else:
                extra_ref[p - n_seq, 2 if which == 0 else 0] = normed
    for p in range(n_seq, heads):
        extra_ref[p - n_seq, 1] = do_ref[:, cols(order_ref[p])]
        extra_ref[p - n_seq, 3] = v_ref[:, cols(order_ref[p])]


def merge_kernel(n_seq, heads, order_ref, main_ref, extra_ref, out_ref, grad_v_ref):
    for p in range(heads):
        at = cols(order_ref[p])
        out_ref[:, at] = main_ref[p, 0] if p < n_seq else extra_ref[p - n_seq, 0]
        grad_v_ref[:, at] = main_ref[p, 1] if p < n_seq else extra_ref[p - n_seq, 3]


def norm_back_kernel(n_seq, heads, order_ref, dqk_ref, extra_ref, q_ref, k_ref, gain_ref, gq_ref, gk_ref):
    scale = 1.0 / (heads * head_width)
    for which, x_ref, out_ref in ((0, q_ref, gq_ref), (1, k_ref, gk_ref)):

        def pieces(p):
            at = cols(order_ref[p])
            up = dqk_ref[p, which] if p < n_seq else extra_ref[p - n_seq, 1 + which]
            gain = gain_ref[which : which + 1, at].astype(f32)
            return at, x_ref[:, at].astype(f32), gain * up.astype(f32)

        squares = jnp.zeros(block, f32)
        inner = jnp.zeros(block, f32)
        for p in range(heads):
            at, x, weighted = pieces(p)
            squares += x * x
            inner += weighted * x
        inverse = lax.rsqrt(jnp.sum(squares, axis=1, keepdims=True) * scale + norm_eps)
        pull = inverse * inverse * inverse * (jnp.sum(inner, axis=1, keepdims=True) * scale)
        inverse = jnp.broadcast_to(inverse, block)
        pull = jnp.broadcast_to(pull, block)
        for p in range(heads):
            at, x, weighted = pieces(p)
            out_ref[:, at] = (inverse * weighted - x * pull).astype(bf16)


def fold_rows(values, combine):
    return combine(values.reshape(values.shape[0] // 8, 8, values.shape[1]), axis=0)


def attention_kernel(parts, most, n_query, n_tiles, group, at, *refs):
    names = ["table", *at["operands"], *at["results"], *at["scratch"]]
    r = dict(zip(names, refs))
    table = r["table"]
    stride = most + 1
    score_scale = log2e / math.sqrt(head_width)
    grad_scale = 1.0 / math.sqrt(head_width)
    key, value, query_of, grad_of = (
        functools.partial(at[k], r) for k in ("key", "value", "query", "grad")
    )
    forward, backward = "forward" in parts, "backward" in parts

    if "prologue" in at:
        at["prologue"](r)
    ahead = at["ahead"]

    @pl.loop(0, n_tiles // unrolled)
    def _(step):
        for t in [step * unrolled + u for u in range(unrolled)]:
            if forward:
                r["dv"][t] = jnp.zeros(block, f32)
            if backward:
                r["dk"][t] = jnp.zeros(block, f32)
            if forward and ahead:
                r["vt"][t] = value(t).T
            if backward and ahead:
                r["kt"][t] = key(t).T

    if backward:
        r["sums"][...] = jnp.zeros(r["sums"].shape, f32)

    def turned(name, t):
        if ahead:
            return r[name][t]
        return (value(t) if name == "vt" else key(t)).T

    def body(count, tiles, counts):
        for a, (i, n) in enumerate(zip(tiles, counts)):
            query, grad = query_of(i), grad_of(i)
            listed = [table[i * stride + j] for j in range(count)]

            def scores(j):
                s = dot(key(listed[j]), query, (1, 1)) * score_scale
                return jnp.where(j < n, s, masked_out) if j else s

            if forward:
                scratch = r["scores"]
                high = None
                for j in range(count):
                    s = scores(j)
                    scratch[a, j] = s
                    peak = fold_rows(s, jnp.max)
                    high = peak if high is None else jnp.maximum(high, peak)
                high = jnp.max(high, axis=0, keepdims=True)
                total = None
                for j in range(count):
                    p = jnp.exp2(scratch[a, j] - high)
                    scratch[a, j] = p
                    part = fold_rows(p, jnp.sum)
                    total = part if total is None else total + part
                total = jnp.sum(total, axis=0, keepdims=True)
                r["lse"][pl.ds(i, 1), :] = high * ln2 + jnp.log(total)
                inverse = 1.0 / total
                probs = [(scratch[a, j] * inverse).astype(bf16) for j in range(count)]
                values_t = jnp.concatenate([turned("vt", t) for t in listed], axis=1)
                out_t = dot(values_t, jnp.concatenate(probs, axis=0), (1, 0)).astype(bf16)
                at["store_out"](r, i, out_t.T)
                delta = jnp.sum(grad.T.astype(f32) * out_t.astype(f32), axis=0, keepdims=True)
                for j, t in enumerate(listed):
                    r["dv"][t] += dot(probs[j], grad, (1, 0))
                if not backward:
                    r["delta"][pl.ds(i, 1), :] = delta
            if backward:
                if not forward:
                    delta = r["delta"][pl.ds(i, 1), :]
                    lse = r["lse"][pl.ds(i, 1), :] * log2e
                dscores = []
                for j, t in enumerate(listed):
                    p = r["scores"][a, j] * inverse if forward else jnp.exp2(scores(j) - lse)
                    dp = dot(value(t), grad, (1, 1))
                    ds = (p * (dp - delta)).astype(bf16)
                    dscores.append(ds)
                    r["dk"][t] += dot(ds, query, (1, 0))
                keys_t = jnp.concatenate([turned("kt", t) for t in listed], axis=1)
                dq_t = dot(keys_t, jnp.concatenate(dscores, axis=0), (1, 0)) * grad_scale
                dq = dq_t.astype(bf16).T
                at["store_dq"](r, i, dq)
                r["sums"][0] += fold_rows(dq.astype(f32) * query.astype(f32), jnp.sum)

    @pl.loop(0, n_query // group)
    def _(g):
        tiles = [g * group + a for a in range(group)]
        counts = [table[t * stride + most] for t in tiles]
        top = functools.reduce(jnp.maximum, counts)
        for static_count in range(1, most + 1):

            @pl.when(top == static_count)
            def _():
                body(static_count, tiles, counts)

    def store_grads(t, where):
        if forward:
            at["store_dv"](r, where, r["dv"][t].astype(bf16))
        if backward:
            dk = (r["dk"][t] * grad_scale).astype(bf16)
            at["store_dk"](r, where, dk)
            r["sums"][1] += fold_rows(dk.astype(f32) * key(t).astype(f32), jnp.sum)

    at["epilogue"](r, store_grads)

    if backward:
        for m in range(2):
            r["gains"][m : m + 1, :] = jnp.sum(r["sums"][m], axis=0, keepdims=True)


def setter(name, where):
    def store(r, i, values):
        r[name][where(i)] = values

    return store


def every_tile(n_tiles, r, store):
    @pl.loop(0, n_tiles // unrolled)
    def _(step):
        for u in range(unrolled):
            store(step * unrolled + u, step * unrolled + u)


def load_shifted(n_x, n_z, r):
    x_index = r["table"][r["table"].shape[0] - 1]
    for s in range(n_x):
        x = lax.rem(x_index + n_x - s, n_x)
        source = r["own"] if s == 0 else r[f"kv{s}"]
        for z in range(n_z):
            for m in range(2):
                r["kv"][z * n_x + x, m] = source[z, 2 + m] if s == 0 else source[z, m]


def store_shifted(n_x, n_z, r, store):
    x_index = r["table"][r["table"].shape[0] - 1]
    for s in range(n_x):
        x = lax.rem(x_index + s, n_x)

        @pl.loop(0, n_z)
        def _(z):
            store(z * n_x + x, (s, z))


def store_part(m):
    def store(r, where, values):
        s, z = where
        r[f"part{s}"][z, m] = values

    return store


def collect_kernel(odq_ref, *refs):
    parts, back_ref = refs[:-1], refs[-1]

    @pl.loop(0, back_ref.shape[0])
    def _(z):
        for m in range(2):
            back_ref[z, m] = odq_ref[z, m]
            total = sum(part[z, m].astype(f32) for part in parts)
            back_ref[z, 2 + m] = total.astype(bf16)


def finish_kernel(n_x, n_z, heads, per, order_ref, slot_ref, here_ref, lse_ref, shared_ref, gq_ref, gk_ref, out_ref, sq_ref, sk_ref):
    n_seq = n_x * n_z
    own, f_index = here_ref[0], here_ref[1]
    out_ref[...] = jnp.zeros(out_ref.shape, f32)
    out_ref[lax.rem(slot_ref[order_ref[own]], 2)] = lse_ref[...]

    @pl.loop(0, heads - n_seq)
    def _(e):
        slot = slot_ref[order_ref[n_seq + e]]

        @pl.when(lax.div(slot, 2) == own)
        def _():
            for x in range(n_x):
                for z in range(n_z):
                    row = z * n_x + x
                    out_ref[lax.rem(slot, 2), row : row + 1, :] = shared_ref[e * n_x + x, z : z + 1, :]

    factor = 1.0 / math.sqrt(n_seq * tile_rows * (heads // per))
    for j in range(per):
        position = order_ref[heads + f_index * per + j]
        for m, (gain_ref, out) in enumerate(((gq_ref, sq_ref), (gk_ref, sk_ref))):
            first = shared_ref[jnp.minimum(position, n_seq - 1), n_z + m : n_z + m + 1, :]
            spread = jnp.maximum(position - n_seq, 0) * n_x
            second = sum(shared_ref[spread + x, n_z + 2 + m : n_z + 3 + m, :] for x in range(n_x))
            total = jnp.where(position < n_seq, first, second)
            out[j : j + 1, :] = total / gain_ref[j : j + 1, :].astype(f32) * factor


def after(values, done):
    return lax.optimization_barrier((values, done))[0]


def shards(query_in, key_in, value_in, out_grad, gain_q, gain_k, mask_lists, tile_counts, head_slot):
    n_x, n_z, n_f = lax.axis_size("x"), lax.axis_size("z"), lax.axis_size("fsdp")
    n_seq = n_x * n_z
    x_index, z_index, f_index = lax.axis_index("x"), lax.axis_index("z"), lax.axis_index("fsdp")
    own = z_index * n_x + x_index
    heads, n_tiles, most = mask_lists.shape
    extra = heads - n_seq
    features = heads * head_width
    seq_axes = ("z", "x")
    q2, k2, v2, g2 = (a.reshape(tile_rows, features) for a in (query_in, key_in, value_in, out_grad))

    def swap(values, axes):
        return lax.all_to_all(values, axes, split_axis=0, concat_axis=0, tiled=True)

    order, value_send = call(
        functools.partial(place_kernel, n_seq, heads),
        "place_heads",
        [((2 * heads,), i32), ((n_seq, *block), bf16)],
        [smem, vmem],
        2 * heads,
        scratch=[pltpu.SMEM((2 * n_seq,), i32)],
        smem_outs=(0,),
    )(head_slot, v2)
    value_main = swap(value_send, seq_axes)

    gains = lax.all_gather(jnp.stack([gain_q, gain_k]), "fsdp", axis=1, tiled=True)
    kq_send, extra_send = call(
        functools.partial(norm_kernel, n_seq, heads),
        "normalize",
        [((n_seq, 2, *block), bf16), ((extra, 4, *block), bf16)],
        [smem] + [vmem] * 5,
        6 * heads,
    )(order, q2, k2, v2, g2, gains)
    extra_own = swap(after(extra_send, value_main), "z")
    (grad_send,) = call(
        functools.partial(split_kernel, n_seq),
        "split_heads",
        [((n_seq, *block), bf16)],
        [smem, vmem],
        2 * heads,
    )(order, g2)
    grad_main = swap(after(grad_send, extra_own), seq_axes)

    table = jnp.concatenate([mask_lists, tile_counts[:, :, None]], axis=2)
    table_main = lax.dynamic_index_in_dim(table, order[own], 0, keepdims=False).reshape(-1)
    table_extra = lax.dynamic_index_in_dim(table, order[n_seq + z_index], 0, keepdims=False)
    table_extra = lax.dynamic_index_in_dim(
        table_extra.reshape(n_z, n_x, most + 1), x_index, 1, keepdims=False
    )
    table_extra = jnp.concatenate([table_extra.reshape(-1), x_index[None]])

    def attention(parts, name, n_query, at, outs, n_operands, passes):
        group = 2
        tile_f32 = pltpu.VMEM((n_tiles, *block), f32)
        tile_bf16 = pltpu.VMEM((n_tiles, *block), bf16)
        scratch = {}
        if "forward" in parts:
            scratch |= {"vt": tile_bf16, "dv": tile_f32, "scores": pltpu.VMEM((group, most, *block), f32)}
        if "backward" in parts:
            scratch |= {"kt": tile_bf16, "dk": tile_f32, "sums": pltpu.VMEM((2, 8, head_width), f32)}
        if not at["ahead"]:
            scratch = {n: v for n, v in scratch.items() if n not in ("kt", "vt")}
            scratch["kv"] = pltpu.VMEM((n_tiles, 2, *block), bf16)
        at = {**at, "scratch": list(scratch), "results": list(outs)}
        return call(
            functools.partial(attention_kernel, parts, most, n_query, n_tiles, group, at),
            name,
            list(outs.values()),
            [smem] + [vmem] * n_operands,
            10 * n_tiles,
            flops=n_query * most * passes * 2 * tile_rows * tile_rows * head_width,
            scratch=list(scratch.values()),
        )

    rows_of = lambda n: ((n, tile_rows), f32)

    def shift(values, s):
        return lax.ppermute(values, "x", [(x, (x + s) % n_x) for x in range(n_x)])

    kv_own = extra_own[:, 2:4]
    kv_shifted = [shift(kv_own, s) for s in range(1, n_x)]
    kq_main = swap(after(kq_send, (grad_main, kv_shifted)), seq_axes)
    kv_shifted = after(kv_shifted, grad_main)
    odq_extra, lse_extra, gain_extra, *dkv_parts = attention(
        ("forward", "backward"),
        "attention_second",
        n_z,
        {
            "operands": ["own", *(f"kv{s}" for s in range(1, n_x))],
            "key": lambda r, t: r["kv"][t, 0],
            "value": lambda r, t: r["kv"][t, 1],
            "query": lambda r, i: r["own"][i, 0],
            "grad": lambda r, i: r["own"][i, 1],
            "ahead": False,
            "prologue": functools.partial(load_shifted, n_x, n_z),
            "epilogue": functools.partial(store_shifted, n_x, n_z),
            "store_out": setter("odq", lambda i: (i, 0)),
            "store_dq": setter("odq", lambda i: (i, 1)),
            "store_dk": store_part(0),
            "store_dv": store_part(1),
        },
        {
            "odq": ((n_z, 2, *block), bf16),
            "lse": rows_of(n_z),
            "gains": ((2, head_width), f32),
            **{f"part{s}": ((n_z, 2, *block), bf16) for s in range(n_x)},
        },
        n_x,
        20,
    )(table_extra, extra_own, *kv_shifted)
    dkv_parts = [dkv_parts[0], *(shift(dkv_parts[s], s) for s in range(1, n_x))]
    (extra_back,) = call(
        collect_kernel, "collect", [((n_z, 4, *block), bf16)], [vmem] * (1 + n_x), 8 * n_z
    )(odq_extra, *dkv_parts)
    extra_home = swap(after(extra_back, kq_main), "z")

    main_at = {
        "ahead": True,
        "epilogue": functools.partial(every_tile, n_tiles),
        "key": lambda r, t: r["kq"][t, 0],
        "value": lambda r, t: r["v"][t],
        "query": lambda r, i: r["kq"][i, 1],
        "grad": lambda r, i: r["g"][i],
    }
    odv_main, lse_main, delta_main = attention(
        ("forward",),
        "forward_first",
        n_tiles,
        {
            **main_at,
            "operands": ["kq", "v", "g"],
            "store_out": setter("odv", lambda i: (i, 0)),
            "store_dv": setter("odv", lambda t: (t, 1)),
        },
        {"odv": ((n_tiles, 2, *block), bf16), "lse": rows_of(n_tiles), "delta": rows_of(n_tiles)},
        3,
        10,
    )(table_main, kq_main, value_main, grad_main)
    odv_home = swap(after(odv_main, extra_home), seq_axes)
    dqk_main, gain_main = attention(
        ("backward",),
        "backward_first",
        n_tiles,
        {
            **main_at,
            "operands": ["kq", "v", "g", "lse", "delta"],
            "store_dq": setter("dqk", lambda i: (i, 0)),
            "store_dk": setter("dqk", lambda t: (t, 1)),
        },
        {"dqk": ((n_tiles, 2, *block), bf16), "gains": ((2, head_width), f32)},
        5,
        16,
    )(table_main, kq_main, value_main, grad_main, lse_main, delta_main)
    dqk_home = swap(after(dqk_main, odv_home), seq_axes)

    wide = ((tile_rows, features), bf16)
    attn_out, grad_v = call(
        functools.partial(merge_kernel, n_seq, heads),
        "merge_heads",
        [wide, wide],
        [smem, vmem, vmem],
        4 * heads,
    )(order, odv_home, extra_home)
    grad_q, grad_k = call(
        functools.partial(norm_back_kernel, n_seq, heads),
        "normalize_back",
        [wide, wide],
        [smem] + [vmem] * 5,
        6 * heads,
    )(order, dqk_home, extra_home, q2, k2, gains)

    gain_sums = lax.psum(jnp.concatenate([gain_main, gain_extra]), "fsdp")
    shared = jnp.concatenate([lse_extra, gain_sums, jnp.zeros((4, head_width), f32)])
    shared = lax.all_gather(lax.all_gather(shared, "x", axis=0), "z", axis=0)
    shared = shared.reshape(n_seq, -1, head_width)
    per = heads // n_f
    lse_slots, share_q, share_k = call(
        functools.partial(finish_kernel, n_x, n_z, heads, per),
        "finish",
        [((2, n_tiles, tile_rows), f32), ((per, head_width), f32), ((per, head_width), f32)],
        [smem] * 3 + [vmem] * 4,
        32,
    )(
        order,
        head_slot,
        jnp.stack([own, f_index]),
        lse_main,
        shared,
        gain_q.reshape(per, head_width),
        gain_k.reshape(per, head_width),
    )
    whole = lambda a: a.reshape(1, tile_rows, features)
    return (
        whole(attn_out),
        lse_slots.reshape(1, 2, n_tiles * tile_rows),
        whole(grad_q),
        whole(grad_k),
        whole(grad_v),
        share_q.reshape(-1),
        share_k.reshape(-1),
    )


def solution(mesh):
    n_seq, n_f = mesh.devices.shape
    n_z = 8
    grid = Mesh(mesh.devices.reshape(n_z, n_seq // n_z, n_f), ("z", "x", "fsdp"))
    rows = P("fsdp", ("z", "x"), None)
    in_specs = (rows,) * 4 + (P("fsdp"),) * 2 + (P(),) * 3
    out_specs = (rows,) * 5 + (P("fsdp"),) * 2
    return jax.shard_map(shards, mesh=grid, in_specs=in_specs, out_specs=out_specs, check_vma=False)
```

time: 1290 us -> 384 us (0.30); the launches traced: 1260 us -> 379 us
  other arithmetic: 363 us -> 2.1 us
  local copies, waits for them, and re-layouts: 259 us -> 19.3 us
  matrix products: 218 us -> 0 us
  waiting for transfers between devices: 233 us -> 129 us
  Pallas kernels: 0 us -> 77.9 us
  blocking collectives: 117 us -> 78.4 us
    scatter-add x32 -> x0, other arithmetic: 286 us -> none  [the longest x16 143 us: block_step(): key_grad = key_grad.at[lists_blk].add(key_part)]
    dot_general x120 -> x0, matrix products: 218 us -> none  [the longest x32 59.6 us: masked_scores(): jnp.einsum('gid,gkjd->gikj', query_tiles, key_tiles, preferred_element_ty...]
    all_to_all x8 -> x7, waiting for transfers between devices: 233 us -> 69.3 us  [swap(): return lax.all_to_all(values, axes, split_axis=0, concat_axis=0, tiled=True)]
    gather x64 -> x0, local copies, waits for them, and re-layouts: 110 us -> none  [the longest x32 64 us: block_step(): key_tiles = jnp.take(key_tiles_all, lists_blk, axis=0)]
    pallas_call x0 -> x10, Pallas kernels: none -> 77.9 us  [the longest x1 23.2 us: shards(): attention(('forward', 'backward'), 'attention_second', n_z, {'operands':...]
    ppermute x0 -> x6, waiting for transfers between devices: none -> 59.4 us  [shift(): return lax.ppermute(values, 'x', [(x, (x + s) % n_x) for x in range(n_x)])]
    psum x1, blocking collectives: 67.1 us -> 14.1 us  [shards(): gain_sums = lax.psum(jnp.concatenate([gain_main, gain_extra]), 'fsdp')]
    all_gather x2 -> x3, blocking collectives: 25.8 us -> 64.3 us  [the longest x2 51.1 us: shards(): shared = lax.all_gather(lax.all_gather(shared, 'x', axis=0), 'z', axis=0)]
  transfers between devices with their start and end apart: 8 -> 13, of which waited for: 6 -> 10; matrix products, arithmetic and copies ran while one was open for 64% -> 1% of each run, Pallas kernels for 0% -> 18%
where the time goes in v1:
time: 384 us; the launch traced here: 379 us
  waiting for transfers between devices  129 us (34%)
  blocking collectives  78.4 us (20%)
  Pallas kernels  77.9 us (20%)
  starting transfers between devices  67.2 us (18%)
  local copies, waits for them, and re-layouts  19.3 us (5%)
  between operations  4.98 us (1%)
    all_to_all x7, waiting for transfers between devices, swap(): return lax.all_to_all(values, axes, split_axis=0, concat_axis=0, tiled=True)  69.3 us
    all_to_all x7, starting transfers between devices, swap(): return lax.all_to_all(values, axes, split_axis=0, concat_axis=0, tiled=True)  60.9 us
    ppermute x6, waiting for transfers between devices, shift(): return lax.ppermute(values, 'x', [(x, (x + s) % n_x) for x in range(n_x)])  59.4 us
    all_gather x2, blocking collectives, shards(): shared = lax.all_gather(lax.all_gather(shared, 'x', axis=0), 'z', axis=0)  51.1 us
    pallas_call x1, Pallas kernels, shards(): attention(('forward', 'backward'), 'attention_second', n_z, {'operands':...  23.2 us
    pallas_call x1, Pallas kernels, shards(): attention(('backward',), 'backward_first', n_tiles, {**main_at, 'operands...  20.9 us
    unnamed x43, local copies, waits for them, and re-layouts  17.5 us
    pallas_call x1, Pallas kernels, shards(): attention(('forward',), 'forward_first', n_tiles, {**main_at, 'operands':...  16.1 us
  transfers between devices with their start and end apart: 13, of which 10 were waited for; matrix products, arithmetic and copies ran while one was open for 1% of the time, Pallas kernels for 18%

profile of v1, /device:TPU:4, one launch (start us, length us, event | category | flops | bytes accessed | tf_op | source)
XLA Modules:
  0.0 378.7 jit_solution(4719456415090905507)
XLA Ops:
  2.6 2.5 place_heads.1
  6.1 11.8 %all-to-all-start = ((bf16[32,128,128]{2,1,0:T(8,128)(2,1)}), bf16[32,128,128]{2,1,0:T(8,128)(2,1)}, u32[]{:S(2)}, u32[]{:S(2)}) async-start(bf16[32,128,128]{2,1,0:T(8,128)(2,1)} %copy-done.12), calls=%async_computation | async-start | bytes 2097152 | tf_op jit(solution)/shard_map/all_to_all | solution.py:360
  18.0 13.2 %all_gather.15.gain_ref = bf16[2,5120]{1,0:T(2,128)(2,1)S(1)} all-gather(bf16[2,640]{1,0:T(2,128)(2,1)S(1)} %pad_maximum_fusion), channel_id=1, replica_groups=mesh['z'=8,'x'=4,'fsdp'=8] {'fsdp'}, dimensions={1}, use_global_device_ids=true | all-gather | bytes 23040 | tf_op jit(solution)/shard_map/all_gather | solution.py:373
  33.8 1.9 normalize.1
  38.0 8.0 %all-to-all-done.refs_2_ = bf16[32,128,128]{2,1,0:T(8,128)(2,1)} async-done(((bf16[32,128,128]{2,1,0:T(8,128)(2,1)}), bf16[32,128,128]{2,1,0:T(8,128)(2,1)}, u32[]{:S(2)}, u32[]{:S(2)}) %all-to-all-start) | async-done | bytes 1048608 | tf_op jit(solution)/shard_map/all_to_all | solution.py:360
  46.0 3.6 all-to-all-start.1
  49.6 1.8 split_heads.1
  51.4 25.5 %all-to-all-done.1.refs_1_ = bf16[8,4,128,128]{3,2,1,0:T(8,128)(2,1)S(1)} async-done(((bf16[8,4,128,128]{3,2,1,0:T(8,128)(2,1)}), bf16[8,4,128,128]{3,2,1,0:T(8,128)(2,1)S(1)}, u32[]{:S(2)}, u32[]{:S(2)}) %all-to-all-start.1) | async-done | bytes 1048608 | tf_op jit(solution)/shard_map/all_to_all | solution.py:360
  76.8 5.0 %all-to-all-start.2 = ((bf16[32,128,128]{2,1,0:T(8,128)(2,1)}), bf16[32,128,128]{2,1,0:T(8,128)(2,1)S(1)}, u32[]{:S(2)}, u32[]{:S(2)}) async-start(bf16[32,128,128]{2,1,0:T(8,128)(2,1)} %split_heads.1), calls=%async_computation.2 | async-start | bytes 2097152 | tf_op jit(solution)/shard_map/all_to_all | solution.py:360
  82.5 2.7 collective-permute-start.1
  85.2 22.0 %collective-permute-done.2.refs_4_ = bf16[8,2,128,128]{3,2,1,0:T(8,128)(2,1)S(1)} collective-permute-done((bf16[8,2,128,128]{3,2,1,0:T(8,128)(2,1)S(1)}, bf16[8,2,128,128]{3,2,1,0:T(8,128)(2,1)S(1)}, u32[]{:S(2)}, u32[]{:S(2)}) %collective-permute-start.2) | collective-permute-done | bytes 524320 | tf_op jit(solution)/shard_map/ppermute | solution.py:425
  107.6 9.5 %collective-permute-done.refs_2_ = bf16[8,2,128,128]{3,2,1,0:T(8,128)(2,1)S(1)} collective-permute-done((bf16[8,2,128,128]{3,2,1,0:T(8,128)(2,1)S(1)}, bf16[8,2,128,128]{3,2,1,0:T(8,128)(2,1)S(1)}, u32[]{:S(2)}, u32[]{:S(2)}) %collective-permute-start) | collective-permute-done | bytes 524320 | tf_op jit(solution)/shard_map/ppermute | solution.py:425
  117.9 10.2 %all-to-all-start.3 = ((bf16[32,2,128,128]{3,2,1,0:T(8,128)(2,1)}), bf16[32,2,128,128]{3,2,1,0:T(8,128)(2,1)}, u32[]{:S(2)}, u32[]{:S(2)}) async-start(bf16[32,2,128,128]{3,2,1,0:T(8,128)(2,1)} %copy-done.7), calls=%async_computation.3 | async-start | bytes 4194304 | tf_op jit(solution)/shard_map/all_to_all | solution.py:360
  132.6 1.8 fusion
  136.9 23.2 %attention_second.1 = (bf16[8,2,128,128]{3,2,1,0:T(8,128)(2,1)S(1)}, f32[8,128]{1,0:T(8,128)S(1)}, f32[2,128]{1,0:T(2,128)S(1)}, bf16[8,2,128,128]{3,2,1,0:T(8,1...) custom-call(s32[97]{0:T(128)S(1)} %pad_add_fusion.refs_0_, ...), custom_call_target="tpu_custom_call" | custom-call | flops 7381975040 | bytes 10485760 | tf_op jit(solution)/shard_map/attention_second/pallas_call | solution.py:431
  163.1 16.8 %collective-permute-done.3.refs_1_ = bf16[8,2,128,128]{3,2,1,0:T(8,128)(2,1)S(1)} collective-permute-done((bf16[8,2,128,128]{3,2,1,0:T(8,128)(2,1)S(1)}, bf16[8,2,128,128]{3,2,1,0:T(8,128)(2,1)S(1)}, u32[]{:S(2)}, u32[]{:S(2)}) %collective-permute-start.3) | collective-permute-done | bytes 524320 | tf_op jit(solution)/shard_map/ppermute | solution.py:425
  179.9 10.3 %collective-permute-done.4.refs_2_ = bf16[8,2,128,128]{3,2,1,0:T(8,128)(2,1)S(1)} collective-permute-done((bf16[8,2,128,128]{3,2,1,0:T(8,128)(2,1)S(1)}, bf16[8,2,128,128]{3,2,1,0:T(8,128)(2,1)S(1)}, u32[]{:S(2)}, u32[]{:S(2)}) %collective-permute-start.4) | collective-permute-done | bytes 524320 | tf_op jit(solution)/shard_map/ppermute | solution.py:425
  192.0 5.6 %all-to-all-start.4 = ((bf16[8,4,128,128]{3,2,1,0:T(8,128)(2,1)}), bf16[8,4,128,128]{3,2,1,0:T(8,128)(2,1)S(1)}, u32[]{:S(2)}, u32[]{:S(2)}) async-start(bf16[8,4,128,128]{3,2,1,0:T(8,128)(2,1)} %collect.1), calls=%async_computation.4 | async-start | bytes 2097152 | tf_op jit(solution)/shard_map/all_to_all | solution.py:360
  198.0 16.1 %forward_first.1 = (bf16[32,2,128,128]{3,2,1,0:T(8,128)(2,1)S(1)}, f32[32,128]{1,0:T(8,128)S(1)}, f32[32,128]{1,0:T(8,128)S(1)}) custom-call(s32[384]{0:T(512)S(1)} %reshape.69.refs_0_, bf16[32,2,128,128]{3,2,1,0:T(8,128)(2,1)} %all-to-all-done.3.refs_1_, bf16[32,128,128]{2,1,0:T(8,128)(2,1)} %all-to-all-done.refs_2_, ...), custom_call_target="tpu_custom_call" | custom-call | flops 14763950080 | bytes 10485760 | tf_op jit(solution)/shard_map/forward_first/pallas_call | solution.py:472
  214.1 1.3 copy-done.9
  215.5 9.7 %all-to-all-done.4.extra_ref = bf16[8,4,128,128]{3,2,1,0:T(8,128)(2,1)S(1)} async-done(((bf16[8,4,128,128]{3,2,1,0:T(8,128)(2,1)}), bf16[8,4,128,128]{3,2,1,0:T(8,128)(2,1)S(1)}, u32[]{:S(2)}, u32[]{:S(2)}) %all-to-all-start.4) | async-done | bytes 1048608 | tf_op jit(solution)/shard_map/all_to_all | solution.py:360
  225.2 8.4 %all-to-all-start.5 = ((bf16[32,2,128,128]{3,2,1,0:T(8,128)(2,1)}), bf16[32,2,128,128]{3,2,1,0:T(8,128)(2,1)S(1)}, u32[]{:S(2)}, u32[]{:S(2)}) async-start(bf16[32,2,128,128]{3,2,1,0:T(8,128)(2,1)} %copy-done.9), calls=%async_computation.5 | async-start | bytes 4194304 | tf_op jit(solution)/shard_map/all_to_all | solution.py:360
  234.8 20.9 %backward_first.1 = (bf16[32,2,128,128]{3,2,1,0:T(8,128)(2,1)S(1)}, f32[2,128]{1,0:T(2,128)S(1)}) custom-call(s32[384]{0:T(512)S(1)} %reshape.69.refs_0_, bf16[32,2,128,128]{3,2,1,0:T(8,128)(2,1)} %all-to-all-done.3.refs_1_, bf16[32,128,128]{2,1,0:T(8,128)(2,1)} %all-to-all-done.refs_2_, bf16[32,128,128]{2,1,0:T(8,128)(2,1)S(1)} %copy-done.11, ...), custom_call_target="tpu_custom_call" | custom-call | flops 23622320128 | bytes 10485760 | tf_op jit(solution)/shard_map/backward_first/pallas_call | solution.py:487
  255.7 1.3 copy-done.8
  257.0 26.1 %all-to-all-done.5.main_ref = bf16[32,2,128,128]{3,2,1,0:T(8,128)(2,1)S(1)} async-done(((bf16[32,2,128,128]{3,2,1,0:T(8,128)(2,1)}), bf16[32,2,128,128]{3,2,1,0:T(8,128)(2,1)S(1)}, u32[]{:S(2)}, u32[]{:S(2)}) %all-to-all-start.5) | async-done | bytes 2097184 | tf_op jit(solution)/shard_map/all_to_all | solution.py:360
  283.1 16.4 %all-to-all-start.6 = ((bf16[32,2,128,128]{3,2,1,0:T(8,128)(2,1)}), bf16[32,2,128,128]{3,2,1,0:T(8,128)(2,1)}, u32[]{:S(2)}, u32[]{:S(2)}) async-start(bf16[32,2,128,128]{3,2,1,0:T(8,128)(2,1)} %copy-done.8), calls=%async_computation.6 | async-start | bytes 4194304 | tf_op jit(solution)/shard_map/all_to_all | solution.py:360
  299.7 14.1 %psum.7 = f32[4,128]{1,0:T(4,128)S(1)} all-reduce(f32[4,128]{1,0:T(4,128)S(1)} %pad_maximum_fusion.1), channel_id=1, replica_groups=mesh['z'=8,'x'=4,'fsdp'=8] {'fsdp'}, use_global_device_ids=true, to_apply=%region_0.1 | all-reduce | flops 512 | bytes 4096 | tf_op jit(solution)/shard_map/psum | solution.py:519
  313.9 10.7 %all-gather = f32[64,128]{1,0:T(8,128)S(1)} all-gather(f32[16,128]{1,0:T(8,128)S(1)} %maximum_maximum_fusion), channel_id=2, replica_groups=mesh['z'=8,'x'=4,'fsdp'=8] {'x'}, dimensions={0}, use_global_device_ids=true | all-gather | bytes 40960 | tf_op jit(solution)/shard_map/all_gather | solution.py:521
  324.6 40.4 %all-gather.1.shared_ref = f32[32,16,128]{2,1,0:T(8,128)S(1)} all-gather(f32[4,16,128]{2,1,0:T(8,128)S(1)} %bitcast.30), channel_id=3, replica_groups=mesh['z'=8,'x'=4,'fsdp'=8] {'z'}, dimensions={0}, use_global_device_ids=true | all-gather | bytes 294912 | tf_op jit(solution)/shard_map/all_gather | solution.py:521
  365.0 1.4 finish.1
  367.0 2.8 merge_heads.1
  372.4 6.0 %normalize_back.1 = (bf16[128,5120]{1,0:T(8,128)(2,1)}, bf16[128,5120]{1,0:T(8,128)(2,1)}) custom-call(s32[80]{0:T(128)S(1)} %get-tuple-element.39.order_ref, bf16[32,2,128,128]{3,2,1,0:T(8,128)(2,1)} %all-to-all-done.6.dqk_ref, bf16[8,4,128,128]{3,2,1,0:T(8,128)(2,1)S(1)} %all-to-all-done.4.extra_ref, bf16[128,5120]{1,0:T(8,128)(2,1)S(1)} %bitcast.25, ...), custom_call_target="tpu_custom_call" | custom-call | bytes 7864320 | tf_op jit(solution)/shard_map/normalize_back/pallas_call | solution.py:511
  (68 shorter events, 22.8 us)
Async XLA Ops:
  0.6 1.3 copy-start.1
  2.6 28.5 %copy-start.2 = (bf16[1,128,5120]{2,1,0:T(8,128)(2,1)S(1)}, bf16[1,128,5120]{2,1,0:T(8,128)(2,1)}, u32[]{:S(2)}) copy-start(bf16[1,128,5120]{2,1,0:T(8,128)(2,1)} %param.11) | copy-start | bytes 3932164
  5.2 1.0 copy-start.12
  6.1 11.8 %copy-start.15 = (bf16[640]{0:T(1024)(128)(2,1)S(1)}, bf16[640]{0:T(1024)(128)(2,1)}, u32[]{:S(2)}) copy-start(bf16[640]{0:T(1024)(128)(2,1)} %param.13) | copy-start | bytes 3844
  6.1 11.8 %copy-start.14 = (bf16[640]{0:T(1024)(128)(2,1)S(1)}, bf16[640]{0:T(1024)(128)(2,1)}, u32[]{:S(2)}) copy-start(bf16[640]{0:T(1024)(128)(2,1)} %param.14) | copy-start | bytes 3844
  6.1 25.0 %copy-start = (bf16[1,128,5120]{2,1,0:T(8,128)(2,1)S(1)}, bf16[1,128,5120]{2,1,0:T(8,128)(2,1)}, u32[]{:S(2)}) copy-start(bf16[1,128,5120]{2,1,0:T(8,128)(2,1)} %param.12) | copy-start | bytes 3932164
  6.1 39.9 %all-to-all-start = ((bf16[32,128,128]{2,1,0:T(8,128)(2,1)}), bf16[32,128,128]{2,1,0:T(8,128)(2,1)}, u32[]{:S(2)}, u32[]{:S(2)}) async-start(bf16[32,128,128]{2,1,0:T(8,128)(2,1)} %copy-done.12), calls=%async_computation | async-start | bytes 2097152 | tf_op jit(solution)/shard_map/all_to_all | solution.py:360
  31.1 1.3 copy-start.3
  32.5 1.3 copy-start.5
  35.7 1.3 copy-start.7
  37.0 1.0 copy-start.13
  46.0 30.8 %all-to-all-start.1 = ((bf16[8,4,128,128]{3,2,1,0:T(8,128)(2,1)}), bf16[8,4,128,128]{3,2,1,0:T(8,128)(2,1)S(1)}, u32[]{:S(2)}, u32[]{:S(2)}) async-start(bf16[8,4,128,128]{3,2,1,0:T(8,128)(2,1)} %copy-done.13), calls=%async_computation.1 | async-start | bytes 2097152 | tf_op jit(solution)/shard_map/all_to_all | solution.py:360
  76.8 41.0 %all-to-all-start.2 = ((bf16[32,128,128]{2,1,0:T(8,128)(2,1)}), bf16[32,128,128]{2,1,0:T(8,128)(2,1)S(1)}, u32[]{:S(2)}, u32[]{:S(2)}) async-start(bf16[32,128,128]{2,1,0:T(8,128)(2,1)} %split_heads.1), calls=%async_computation.2 | async-start | bytes 2097152 | tf_op jit(solution)/shard_map/all_to_all | solution.py:360
  81.9 25.3 %collective-permute-start.2 = (bf16[8,2,128,128]{3,2,1,0:T(8,128)(2,1)S(1)}, bf16[8,2,128,128]{3,2,1,0:T(8,128)(2,1)S(1)}, u32[]{:S(2)}, u32[]{:S(2)}) collective-permute-start(bf16[8,2,128,128]{3,2,1,0:T(8,128)(2,1)S(1)} %slice.4), channel_id=1, source_target_pairs={{0,24},{8,0},{16,8},{24,16},{1,25},{9,1},{17,9},{25,17},{2,26},{10... | collective-permute-start | bytes 1572872 | tf_op jit(solution)/shard_map/ppermute | solution.py:425
  82.5 25.1 %collective-permute-start.1 = (bf16[8,2,128,128]{3,2,1,0:T(8,128)(2,1)S(1)}, bf16[8,2,128,128]{3,2,1,0:T(8,128)(2,1)S(1)}, u32[]{:S(2)}, u32[]{:S(2)}) collective-permute-start(bf16[8,2,128,128]{3,2,1,0:T(8,128)(2,1)S(1)} %slice.4), channel_id=1, source_target_pairs={{0,16},{8,24},{16,0},{24,8},{1,17},{9,25},{17,1},{25,9},{2,18},{10... | collective-permute-start | bytes 1572872 | tf_op jit(solution)/shard_map/ppermute | solution.py:425
  85.2 31.9 %collective-permute-start = (bf16[8,2,128,128]{3,2,1,0:T(8,128)(2,1)S(1)}, bf16[8,2,128,128]{3,2,1,0:T(8,128)(2,1)S(1)}, u32[]{:S(2)}, u32[]{:S(2)}) collective-permute-start(bf16[8,2,128,128]{3,2,1,0:T(8,128)(2,1)S(1)} %slice.4), channel_id=1, source_target_pairs={{0,8},{8,16},{16,24},{24,0},{1,9},{9,17},{17,25},{25,1},{2,10},{10... | collective-permute-start | bytes 1572872 | tf_op jit(solution)/shard_map/ppermute | solution.py:425
  117.9 80.1 %copy-start.10 = (bf16[32,128,128]{2,1,0:T(8,128)(2,1)}, bf16[32,128,128]{2,1,0:T(8,128)(2,1)S(1)}, u32[]{:S(2)}) copy-start(bf16[32,128,128]{2,1,0:T(8,128)(2,1)S(1)} %all-to-all-done.2.refs_3_) | copy-start | bytes 3145732
  117.9 14.7 %copy-start.20 = (s32[40,32]{0,1:T(8,128)S(1)}, s32[40,32]{0,1:T(8,128)}, u32[]{:S(2)}) copy-start(s32[40,32]{0,1:T(8,128)} %param.16) | copy-start | bytes 15364
  117.9 74.1 %all-to-all-start.3 = ((bf16[32,2,128,128]{3,2,1,0:T(8,128)(2,1)}), bf16[32,2,128,128]{3,2,1,0:T(8,128)(2,1)}, u32[]{:S(2)}, u32[]{:S(2)}) async-start(bf16[32,2,128,128]{3,2,1,0:T(8,128)(2,1)} %copy-done.7), calls=%async_computation.3 | async-start | bytes 4194304 | tf_op jit(solution)/shard_map/all_to_all | solution.py:360
  135.8 1.0 copy-start.19
  160.1 19.8 %collective-permute-start.3 = (bf16[8,2,128,128]{3,2,1,0:T(8,128)(2,1)S(1)}, bf16[8,2,128,128]{3,2,1,0:T(8,128)(2,1)S(1)}, u32[]{:S(2)}, u32[]{:S(2)}) collective-permute-start(bf16[8,2,128,128]{3,2,1,0:T(8,128)(2,1)S(1)} %get-tuple-element.52), channel_id=1, source_target_pairs={{0,8},{8,16},{16,24},{24,0},{1,9},{9,17},{17,25},{25,1},{2,10},{10... | collective-permute-start | bytes 1572872 | tf_op jit(solution)/shard_map/ppermute | solution.py:425
  161.4 28.8 %collective-permute-start.4 = (bf16[8,2,128,128]{3,2,1,0:T(8,128)(2,1)S(1)}, bf16[8,2,128,128]{3,2,1,0:T(8,128)(2,1)S(1)}, u32[]{:S(2)}, u32[]{:S(2)}) collective-permute-start(bf16[8,2,128,128]{3,2,1,0:T(8,128)(2,1)S(1)} %get-tuple-element.53), channel_id=1, source_target_pairs={{0,16},{8,24},{16,0},{24,8},{1,17},{9,25},{17,1},{25,9},{2,18},{10... | collective-permute-start | bytes 1572872 | tf_op jit(solution)/shard_map/ppermute | solution.py:425
  162.2 28.4 %collective-permute-start.5 = (bf16[8,2,128,128]{3,2,1,0:T(8,128)(2,1)S(1)}, bf16[8,2,128,128]{3,2,1,0:T(8,128)(2,1)S(1)}, u32[]{:S(2)}, u32[]{:S(2)}) collective-permute-start(bf16[8,2,128,128]{3,2,1,0:T(8,128)(2,1)S(1)} %get-tuple-element.54), channel_id=1, source_target_pairs={{0,24},{8,0},{16,8},{24,16},{1,25},{9,1},{17,9},{25,17},{2,26},{10... | collective-permute-start | bytes 1572872 | tf_op jit(solution)/shard_map/ppermute | solution.py:425
  192.0 33.2 %all-to-all-start.4 = ((bf16[8,4,128,128]{3,2,1,0:T(8,128)(2,1)}), bf16[8,4,128,128]{3,2,1,0:T(8,128)(2,1)S(1)}, u32[]{:S(2)}, u32[]{:S(2)}) async-start(bf16[8,4,128,128]{3,2,1,0:T(8,128)(2,1)} %collect.1), calls=%async_computation.4 | async-start | bytes 2097152 | tf_op jit(solution)/shard_map/all_to_all | solution.py:360
  214.1 1.3 copy-start.9
  225.2 58.0 %all-to-all-start.5 = ((bf16[32,2,128,128]{3,2,1,0:T(8,128)(2,1)}), bf16[32,2,128,128]{3,2,1,0:T(8,128)(2,1)S(1)}, u32[]{:S(2)}, u32[]{:S(2)}) async-start(bf16[32,2,128,128]{3,2,1,0:T(8,128)(2,1)} %copy-done.9), calls=%async_computation.5 | async-start | bytes 4194304 | tf_op jit(solution)/shard_map/all_to_all | solution.py:360
  233.6 1.2 copy-start.11
  255.7 1.4 copy-start.8
  283.1 81.9 %copy-start.17 = (s32[40]{0:T(128)S(1)}, s32[40]{0:T(128)}, u32[]{:S(2)}) copy-start(s32[40]{0:T(128)} %slot_ref.3) | copy-start | bytes 484
  283.1 86.7 %all-to-all-start.6 = ((bf16[32,2,128,128]{3,2,1,0:T(8,128)(2,1)}), bf16[32,2,128,128]{3,2,1,0:T(8,128)(2,1)}, u32[]{:S(2)}, u32[]{:S(2)}) async-start(bf16[32,2,128,128]{3,2,1,0:T(8,128)(2,1)} %copy-done.8), calls=%async_computation.6 | async-start | bytes 4194304 | tf_op jit(solution)/shard_map/all_to_all | solution.py:360
  369.8 1.3 copy-start.4
  371.1 1.3 copy-start.6
  (2 other events, 1.4 us)
